TPU v7x, 768 devices: a whole 4x8x12 slice. The times are simulated.
768 devices in a mesh: col: 24 (over z, core), row: 32 (over y, x).
Axes of the slice: x: 4, y: 8, z: 12, core: 2. Of those that a mesh axis runs over, the one named last changes fastest.
Arguments:
- features: bfloat16 [768, 294912], P('col', 'row'), may hold values from -6 to 6
- adj_values: bfloat16 [2304, 4, 128, 128], P('row'), may hold values from -0.25 to 0.25
- neighbours: int32 [2304, 4], P('row'), may hold values from 0 to 71, as said below
- counts: int32 [2304], P('row'), may hold values from 1 to 4, as said below
- labels: int32 [294912], P('row'), may hold values from 0 to 152
- layer_weight: bfloat16 [768, 1024], replicated, may hold values from -0.21875 to 0.21875
- label_embed: bfloat16 [153, 1024], replicated, may hold values from -6 to 6
Outputs:
- weight_grad: float32 [768, 1024], P('col')
- feature_grad: bfloat16 [768, 294912], P('col', 'row')
Inputs may be any that keep to these rules, and one draw needn't show every extreme that they name: `neighbours`: each row holds 4 different block numbers of its own slab, the first being the row block's own number within the slab. `counts`: slots at or past the count are padding and carry no edges.
All inputs are finite; a program needn't handle non-finite values.
Results may differ from a plain program's by a relative error of at most 0.013.
Values may be sent and summed in bfloat16 or wider, within the bound.
A program may use at most 64 MiB of HBM per device.

v0:
```python
import math

import jax
import jax.numpy as jnp
from jax import lax
from jax.sharding import PartitionSpec as P


def shards(features, adj_values, neighbours, counts, labels, layer_weight, label_embed):
    fin_dev, slab_nodes = features.shape
    block_count, slot_count, block_size, _ = adj_values.shape
    col_count = lax.axis_size("col")
    own_nodes = slab_nodes // col_count
    live_mask = jnp.arange(slot_count, dtype=jnp.int32)[None, :] < counts[:, None]
    blocks = features.reshape(fin_dev, block_count, block_size)
    picked = jnp.take(blocks, neighbours.reshape(-1), axis=1).reshape(
        fin_dev, block_count, slot_count, block_size
    )
    picked = picked * live_mask[None, :, :, None].astype(jnp.bfloat16)
    summed = jnp.einsum("fiks,iksd->fid", picked, adj_values, preferred_element_type=jnp.float32)
    aggregate = summed.reshape(fin_dev, slab_nodes).astype(jnp.bfloat16)
    regrouped = lax.all_to_all(aggregate, "col", split_axis=1, concat_axis=0, tiled=True)
    hidden = lax.dot_general(
        layer_weight, regrouped, (((0,), (0,)), ((), ())), preferred_element_type=jnp.float32
    )
    sigma = jax.nn.sigmoid(hidden)
    derivative = sigma * (1.0 + hidden * (1.0 - sigma))
    own_labels = lax.dynamic_slice_in_dim(labels, lax.axis_index("col") * own_nodes, own_nodes)
    class_count = label_embed.shape[0]
    one_hot = (own_labels[None, :] == jnp.arange(class_count, dtype=jnp.int32)[:, None]).astype(
        jnp.bfloat16
    )
    target = lax.dot_general(
        label_embed, one_hot, (((0,), (0,)), ((), ())), preferred_element_type=jnp.float32
    )
    grad_hidden = (derivative * target).astype(jnp.bfloat16)
    weight_part = lax.dot_general(
        regrouped, grad_hidden, (((1,), (1,)), ((), ())), preferred_element_type=jnp.float32
    )
    grad_aggregate = jnp.dot(layer_weight, grad_hidden, preferred_element_type=jnp.float32).astype(
        jnp.bfloat16
    )
    returned = lax.all_to_all(grad_aggregate, "col", split_axis=0, concat_axis=1, tiled=True)
    grad_blocks = returned.reshape(fin_dev, block_count, block_size)
    contribution = jnp.einsum(
        "fid,iksd->fiks", grad_blocks, adj_values, preferred_element_type=jnp.float32
    )
    contribution = contribution * live_mask[None, :, :, None].astype(jnp.float32)
    flat_terms = contribution.reshape(fin_dev, block_count * slot_count, block_size)
    upper_part = flat_terms.astype(jnp.bfloat16)
    lower_part = (flat_terms - upper_part.astype(jnp.float32)).astype(jnp.bfloat16)
    scatter_table = (
        neighbours.reshape(-1)[:, None] == jnp.arange(block_count, dtype=jnp.int32)[None, :]
    ).astype(jnp.bfloat16)
    feature_sum = jnp.einsum(
        "pb,fps->fbs", scatter_table, upper_part, preferred_element_type=jnp.float32
    )
    feature_sum = feature_sum + jnp.einsum(
        "pb,fps->fbs", scatter_table, lower_part, preferred_element_type=jnp.float32
    )
    feature_grad = feature_sum.reshape(fin_dev, slab_nodes).astype(jnp.bfloat16)
    factor = 1.0 / math.sqrt(slab_nodes * lax.axis_size("row"))
    summed_grad = lax.psum(weight_part, ("col", "row"))
    weight_rows = lax.dynamic_slice_in_dim(summed_grad, lax.axis_index("col") * fin_dev, fin_dev, 0)
    return (weight_rows * factor, feature_grad)


def solution(mesh):
    return jax.shard_map(
        shards,
        mesh=mesh,
        in_specs=(
            P("col", "row"),
            P("row", None, None, None),
            P("row", None),
            P("row"),
            P("row"),
            P(),
            P(),
        ),
        out_specs=(P("col", None), P("col", "row")),
        check_vma=False,
    )
```

profile of v0, /device:TPU:1, one launch (start us, length us, event | category | flops | bytes accessed | tf_op | source)
XLA Modules:
  0.0 585.3 jit_solution(11489752715588547353)
XLA Ops:
  7.2 0.0 copy-start
  7.2 0.8 compare_and_fusion
  8.0 0.8 copy.35
  8.8 0.0 copy-start.1
  8.8 0.1 copy.34
  8.9 0.1 reshape.112
  9.0 0.3 copy-done.1
  9.4 1.3 fusion.33
  10.7 1.2 copy_bitcast_fusion.1
  11.9 2.9 gather_fusion
  14.8 6.0 %fusion.20 = bf16[32,72,128]{2,0,1:T(8,128)(2,1)S(1)} fusion(bf16[72,4,128,128]{3,2,1,0:T(8,128)(2,1)} %param.8, bf16[32,72,4,128]{3,0,2,1:T(8,128)(2,1)} %bitcast.73, pred[72,4]{1,0:T(8,128)(4,1)S(1)} %copy.34, bf16[72,4]{1,0:T(8,128)(2,1)S(1)} %get-tuple-element.3), kind=kOutput, calls=%fused_computation.24 | convolution fusion | flops 304644096 | bytes 12387168 | tf_op jit(solution)/shard_map/fiks,iksd->fid/dot_general | solution.py:20
  20.8 0.2 copy.37
  21.1 0.3 convert_element_type.58
  21.4 0.9 copy.38
  22.3 16.7 %all-to-all-start = ((bf16[32,24,384]{2,0,1:T(8,128)(2,1)}), bf16[32,24,384]{2,0,1:T(8,128)(2,1)S(1)}, u32[]{:S(2)}, u32[]{:S(2)}) async-start(bf16[32,24,384]{2,0,1:T(8,128)(2,1)} %copy.38), calls=%async_computation | async-start | bytes 1179648 | tf_op jit(solution)/shard_map/all_to_all | solution.py:22
  39.0 0.8 dynamic_slice.6
  39.7 24.0 %all-to-all-done = bf16[32,24,384]{2,0,1:T(8,128)(2,1)S(1)} async-done(((bf16[32,24,384]{2,0,1:T(8,128)(2,1)}), bf16[32,24,384]{2,0,1:T(8,128)(2,1)S(1)}, u32[]{:S(2)}, u32[]{:S(2)}) %all-to-all-start) | async-done | bytes 589856 | tf_op jit(solution)/shard_map/all_to_all | solution.py:22
  63.8 0.0 copy-done
  63.8 0.0 copy-start.4
  63.8 0.8 fusion.37
  64.6 0.2 copy-done.4
  64.8 0.7 fusion.6
  65.5 0.8 fusion.23
  66.3 1.1 copy.39
  67.4 5.8 all-to-all-start.1
  73.2 0.2 all-reduce.2.cloned.1.call-start
  73.4 2.7 fusion.38
  76.1 0.0 copy-start.2
  76.1 0.0 copy-start.3
  76.1 0.0 all-reduce.2.cloned.1.call-update
  76.1 0.7 copy-done.2
  76.8 0.1 reshape.115
  77.0 487.3 %all-reduce.2.cloned.1.call-done = f32[768,1024]{1,0:T(8,128)} async-done(((f32[768,1024]{1,0:T(8,128)}), f32[768,1024]{1,0:T(8,128)}) %all-reduce.2.cloned.1.call-update) | async-done | bytes 3145744 | tf_op jit(solution)/shard_map/psum | solution.py:63
  564.2 1.6 dynamic-slice_multiply_fusion
  565.8 0.0 all-to-all-done.1
  565.8 0.2 copy.40
  566.0 0.3 reshape.113
  566.3 0.0 copy-done.3
  566.3 5.8 broadcast_multiply_fusion
  572.1 2.7 fusion
  574.8 2.7 fusion.16
  577.6 0.9 copy.65
  (2 shorter events, 0.0 us)
Async XLA Ops:
  7.2 56.6 %copy-start = (bf16[768,1024]{1,0:T(8,128)(2,1)S(1)}, bf16[768,1024]{1,0:T(8,128)(2,1)}, u32[]{:S(2)}) copy-start(bf16[768,1024]{1,0:T(8,128)(2,1)} %param.12) | copy-start | bytes 4718596
  8.8 0.6 copy-start.1
  22.3 41.5 %all-to-all-start = ((bf16[32,24,384]{2,0,1:T(8,128)(2,1)}), bf16[32,24,384]{2,0,1:T(8,128)(2,1)S(1)}, u32[]{:S(2)}, u32[]{:S(2)}) async-start(bf16[32,24,384]{2,0,1:T(8,128)(2,1)} %copy.38), calls=%async_computation | async-start | bytes 1179648 | tf_op jit(solution)/shard_map/all_to_all | solution.py:22
  63.8 1.0 copy-start.4
  67.4 498.4 %all-to-all-start.1 = ((bf16[24,32,384]{2,1,0:T(8,128)(2,1)}), bf16[24,32,384]{2,1,0:T(8,128)(2,1)S(1)}, u32[]{:S(2)}, u32[]{:S(2)}) async-start(bf16[24,32,384]{2,1,0:T(8,128)(2,1)} %bitcast.11), calls=%async_computation.1 | async-start | bytes 1179648 | tf_op jit(solution)/shard_map/all_to_all | solution.py:43
  73.2 491.1 %all-reduce.2.cloned.1.call-start = ((), (), s32[]{:S(2)}) async-start(), calls=%async_computation.2 | async-start | bytes 6291456 | tf_op jit(solution)/shard_map/psum | solution.py:63
  76.1 0.8 copy-start.2
  76.1 490.2 %copy-start.3 = (f32[72,4]{1,0:T(8,128)S(1)}, f32[72,4]{1,0:T(8,128)}, u32[]{:S(2)}) copy-start(f32[72,4]{1,0:T(8,128)} %get-tuple-element.2) | copy-start | bytes 3460
Sparse Core Ops, SparseCore 0:
  79.4 484.8 all-reduce.1
where the time goes:
time: 586 us; the launch traced here: 585 us
  waiting for transfers between devices  511 us (87%)
  starting transfers between devices  22.7 us (4%)
  matrix products  22.3 us (4%)
  between operations  14.2 us (2%)
  local copies, waits for them, and re-layouts  11.1 us (2%)
    psum x1, waiting for transfers between devices, shards(): summed_grad = lax.psum(weight_part, ('col', 'row'))  487 us
    all_to_all x1, waiting for transfers between devices, shards(): lax.all_to_all(aggregate, 'col', split_axis=1, concat_axis=0, tiled=True)  24 us
    all_to_all x1, starting transfers between devices, shards(): lax.all_to_all(aggregate, 'col', split_axis=1, concat_axis=0, tiled=True)  16.7 us
  transfers between devices with their start and end apart: 3, of which 2 were waited for; matrix products, arithmetic and copies ran while one was open for 1% of the time, Pallas kernels for 0%

commit v1 on v0

v1 whole, which is shorter than its diff:
```python
import functools
import math

import jax
import jax.numpy as jnp
from jax import lax
from jax.experimental import pallas as pl
from jax.experimental.pallas import tpu as pltpu
from jax.sharding import PartitionSpec as P

NX = 4
BF16, F32 = jnp.bfloat16, jnp.float32
MESH = pl.DeviceIdType.MESH
VMEM_LIMIT = 56 * 1024 * 1024


def exchange_kernel(
    col_count,
    row_count,
    factor,
    nbr_ref,
    cnt_ref,
    x_ref,
    lab_ref,
    le_ref,
    adj_hbm,
    w_hbm,
    ret_ref,
    wg_ref,
    x_blocks,
    adj,
    w,
    agg,
    rg,
    gh,
    ga,
    wp,
    core_out,
    core_in,
    x_out,
    x_in,
    q_own,
    y_out,
    y_in,
    z_out,
    z_in,
    y_all,
    x_all,
    adj_sem,
    w_sem,
    own_sem,
    fwd_send,
    fwd_recv,
    bwd_send,
    bwd_recv,
    red_send,
    red_recv,
):
    parts = agg.shape[0]
    fin_dev = x_ref.shape[0]
    fin, fout = w.shape
    slots = nbr_ref.shape[1]
    blk = x_ref.shape[1] // nbr_ref.shape[0]
    ny, nz = row_count // NX, col_count // 2
    rows_x, cols_y = fin_dev // NX, fout // ny
    classes = le_ref.shape[0]

    col, row = lax.axis_index("col"), lax.axis_index("row")
    z, core = col // 2, lax.rem(col, 2)
    y, x = row // NX, lax.rem(row, NX)

    def col_peer(s):
        return lax.rem(col + s, col_count)

    def x_peer(s):
        return y * NX + lax.rem(x + s, NX)

    def y_peer(s):
        return lax.rem(y + s, ny) * NX + x

    barrier = pltpu.get_barrier_semaphore()

    def greet_col(s, c):
        pl.semaphore_signal(barrier, inc=1, device_id={"col": col_peer(s)}, device_id_type=MESH)
        return c

    lax.fori_loop(1, col_count, greet_col, 0)
    for s in range(1, NX):
        pl.semaphore_signal(barrier, inc=1, device_id={"row": x_peer(s)}, device_id_type=MESH)
    for s in range(1, ny):
        pl.semaphore_signal(barrier, inc=1, device_id={"row": y_peer(s)}, device_id_type=MESH)

    pieces = adj_sem.shape[1]
    width = col_count // pieces

    def adj_copy(b, g):
        at = pl.ds(g * width, width)
        return pltpu.make_async_copy(adj_hbm.at[at, b], adj.at[b, at], adj_sem.at[b, g])

    for b in range(parts):
        for g in range(pieces):
            adj_copy(b, g).start()
    w_copy = pltpu.make_async_copy(w_hbm, w, w_sem)
    w_copy.start()

    for k in range(nbr_ref.shape[0]):
        x_blocks[k] = x_ref[:, k * blk : (k + 1) * blk]

    def aggregate(b, g):
        adj_copy(b, g).wait()

        def one(d, c):
            i = d * parts + b
            count = cnt_ref[i]
            picked = []
            for k in range(slots):
                live = jnp.clip(count - k, 0, 1).astype(F32)
                picked.append(x_blocks[nbr_ref[i, k]] * jnp.full((fin_dev, blk), live).astype(BF16))
            total = jnp.dot(
                jnp.concatenate(picked, axis=1), adj[b, d], preferred_element_type=F32
            )
            agg[b, d] = total.astype(BF16)
            return c

        for t in range(width):
            one(g * width + t, 0)

    def send_forward(b):
        def one(s, c):
            d = col_peer(s)
            pltpu.make_async_remote_copy(
                agg.at[b, d],
                rg.at[b, pl.ds(col * fin_dev, fin_dev)],
                fwd_send,
                fwd_recv.at[b],
                device_id={"col": d},
                device_id_type=MESH,
            ).start()
            return c

        lax.fori_loop(1, col_count, one, 0)

    for b in range(parts):
        lax.fori_loop(0, pieces, lambda g, c, b=b: (aggregate(b, g), c)[1], 0)
        if b == 0:
            pl.semaphore_wait(barrier, (col_count - 1) + (NX - 1) + (ny - 1))
        send_forward(b)
        rg[b, pl.ds(pl.multiple_of(col * fin_dev, fin_dev), fin_dev), :] = agg[b, col]

    w_copy.wait()
    tile = min(256, fout)

    def node_part(b, c):
        got = rg.at[b, pl.ds(0, fin - fin_dev)]
        pltpu.make_async_copy(got, got, fwd_recv.at[b]).wait()
        rows = rg[b]
        label = lab_ref[pl.ds(col * parts + b, 1), :]
        one_hot = jnp.where(
            lax.broadcasted_iota(jnp.int32, (classes, blk), 0) == label, 1.0, 0.0
        ).astype(BF16)
        for j in range(fout // tile):
            at = pl.ds(j * tile, tile)
            hidden = lax.dot_general(
                rows, w[:, at], (((0,), (0,)), ((), ())), preferred_element_type=F32
            )
            target = lax.dot_general(
                one_hot, le_ref[:, at], (((0,), (0,)), ((), ())), preferred_element_type=F32
            )
            sigma = 1.0 / (1.0 + jnp.exp(-hidden))
            slope = sigma * (1.0 + hidden * (1.0 - sigma))
            gh[b, :, at] = (slope * target).astype(BF16)
        grad = gh[b]
        step = min(256, fin)
        for m in range(fin // step):
            part = lax.dot_general(
                w[pl.ds(m * step, step), :],
                grad,
                (((1,), (1,)), ((), ())),
                preferred_element_type=F32,
            ).astype(BF16)
            per = step // fin_dev
            ga[b, pl.ds(m * per, per)] = part.reshape(per, fin_dev, blk)

        def send(s, c):
            d = col_peer(s)
            pltpu.make_async_remote_copy(
                ga.at[b, d],
                ret_ref.at[col * parts + b],
                bwd_send,
                bwd_recv,
                device_id={"col": d},
                device_id_type=MESH,
            ).start()
            return c

        lax.fori_loop(1, col_count, send, 0)
        pltpu.make_async_copy(ga.at[b, col], ret_ref.at[col * parts + b], own_sem.at[b]).start()
        return c

    lax.fori_loop(0, parts, node_part, 0)

    left = jnp.concatenate([rg[b] for b in range(parts)], axis=1)

    def weight_part(j, c):
        at = pl.ds(pl.multiple_of(j * tile, tile), tile)
        right = jnp.concatenate([gh[b, :, at] for b in range(parts)], axis=0)
        part = jnp.dot(left, right, preferred_element_type=F32)
        wp[:, :, :, at] = part.reshape(nz, 2, fin_dev, tile)
        return c

    lax.fori_loop(0, fout // tile, weight_part, 0)

    def round_core(i, c):
        core_out[i] = wp[i, 1 - core].astype(BF16)
        return c

    lax.fori_loop(0, nz, round_core, 0)
    to_core = pltpu.make_async_remote_copy(
        core_out,
        core_in,
        red_send.at[0],
        red_recv.at[0],
        device_id={"col": z * 2 + 1 - core},
        device_id_type=MESH,
    )
    to_core.start()
    to_core.wait_recv()

    pair = 16 // rows_x

    def round_x(i, c):
        sums = []
        for t in range(pair):
            total = wp[i * pair + t, core] + core_in[i * pair + t].astype(F32)
            wp[i * pair + t, core] = total
            sums.append(total)
        for k in range(NX):
            piece = jnp.concatenate([v[k * rows_x : (k + 1) * rows_x] for v in sums], axis=0)
            x_out[k, pl.ds(pl.multiple_of(i * 16, 16), 16), :] = piece.astype(BF16)
        return c

    lax.fori_loop(0, nz // pair, round_x, 0)
    for s in range(1, NX):
        pltpu.make_async_remote_copy(
            x_out.at[lax.rem(x + s, NX)],
            x_in.at[s - 1],
            red_send.at[1],
            red_recv.at[1],
            device_id={"row": x_peer(s)},
            device_id_type=MESH,
        ).start()
    pltpu.make_async_copy(x_in, x_in, red_recv.at[1]).wait()

    def round_y(i, c):
        at = pl.ds(pl.multiple_of(i * 16, 16), 16)
        own = pl.ds(pl.multiple_of(x * rows_x, rows_x), rows_x)
        total = jnp.concatenate([wp[i * pair + t, core, own, :] for t in range(pair)], axis=0)
        for s in range(NX - 1):
            total = total + x_in[s, at, :].astype(F32)
        for k in range(ny):
            piece = total[:, k * cols_y : (k + 1) * cols_y]
            q_own[k, at, :] = piece
            y_out[k, at, :] = piece.astype(BF16)
        return c

    lax.fori_loop(0, nz // pair, round_y, 0)

    def send_y(s, c):
        pltpu.make_async_remote_copy(
            y_out.at[lax.rem(y + s, ny)],
            y_in.at[s - 1],
            red_send.at[2],
            red_recv.at[2],
            device_id={"row": y_peer(s)},
            device_id_type=MESH,
        ).start()
        return c

    lax.fori_loop(1, ny, send_y, 0)
    pltpu.make_async_copy(y_in, y_in, red_recv.at[2]).wait()

    total = q_own[y]
    for s in range(ny - 1):
        total = total + y_in[s].astype(F32)
    z_out[...] = total.reshape(nz, rows_x, cols_y)

    def send_z(s, c):
        other = lax.rem(z + s, nz)
        pltpu.make_async_remote_copy(
            z_out.at[other],
            z_in.at[s - 1],
            red_send.at[3],
            red_recv.at[3],
            device_id={"col": other * 2 + core},
            device_id_type=MESH,
        ).start()
        return c

    lax.fori_loop(1, nz, send_z, 0)
    pltpu.make_async_copy(z_in, z_in, red_recv.at[3]).wait()
    total = z_out[z]
    for s in range(nz - 1):
        total = total + z_in[s]
    y_all[y] = total * factor

    def share_y(s, c):
        pltpu.make_async_remote_copy(
            y_all.at[y],
            y_all.at[y],
            red_send.at[4],
            red_recv.at[4],
            device_id={"row": y_peer(s)},
            device_id_type=MESH,
        ).start()
        return c

    lax.fori_loop(1, ny, share_y, 0)
    got = y_all.at[pl.ds(0, ny - 1)]
    pltpu.make_async_copy(got, got, red_recv.at[4]).wait()
    x_all[x] = jnp.concatenate([y_all[k] for k in range(ny)], axis=1)
    for s in range(1, NX):
        pltpu.make_async_remote_copy(
            x_all.at[x],
            x_all.at[x],
            red_send.at[5],
            red_recv.at[5],
            device_id={"row": x_peer(s)},
            device_id_type=MESH,
        ).start()
    got = x_all.at[pl.ds(0, NX - 1)]
    pltpu.make_async_copy(got, got, red_recv.at[5]).wait()
    wg_ref[...] = x_all[...].reshape(fin_dev, fout)

    got = ret_ref.at[pl.ds(0, (col_count - 1) * parts)]
    pltpu.make_async_copy(got, got, bwd_recv).wait()
    for b in range(parts):
        pltpu.make_async_copy(ga.at[b, col], ret_ref.at[col * parts + b], own_sem.at[b]).wait()
    sent = agg.at[:, pl.ds(0, col_count - 1)]
    pltpu.make_async_copy(sent, sent, fwd_send).wait()
    sent = ga.at[:, pl.ds(0, col_count - 1)]
    pltpu.make_async_copy(sent, sent, bwd_send).wait()
    to_core.wait_send()
    pltpu.make_async_copy(x_in, x_in, red_send.at[1]).wait()
    pltpu.make_async_copy(y_in, y_in, red_send.at[2]).wait()
    pltpu.make_async_copy(z_in, z_in, red_send.at[3]).wait()
    sent = y_all.at[pl.ds(0, ny - 1)]
    pltpu.make_async_copy(sent, sent, red_send.at[4]).wait()
    sent = x_all.at[pl.ds(0, NX - 1)]
    pltpu.make_async_copy(sent, sent, red_send.at[5]).wait()


def spread_kernel(nbr_ref, cnt_ref, ga_ref, adj_hbm, out_ref, adj, acc, adj_sem):
    blocks, slots = nbr_ref.shape
    fin_dev, blk = ga_ref.shape[1:]
    pieces = adj_sem.shape[0]
    width = blocks // pieces

    def adj_copy(g):
        at = pl.ds(g * width, width)
        return pltpu.make_async_copy(adj_hbm.at[at], adj.at[at], adj_sem.at[g])

    for g in range(pieces):
        adj_copy(g).start()
    acc[...] = jnp.zeros_like(acc)

    def piece(g, c):
        adj_copy(g).wait()
        terms = []
        for t in range(width):
            i = g * width + t
            terms.append(
                lax.dot_general(
                    ga_ref[i], adj[i], (((1,), (1,)), ((), ())), preferred_element_type=F32
                )
            )
        for t in range(width):
            i = g * width + t
            count = cnt_ref[i]
            for k in range(slots):
                term = terms[t][:, k * blk : (k + 1) * blk]
                at = nbr_ref[i, k]
                acc[at] = acc[at] + jnp.where(k < count, term, jnp.zeros_like(term))
        return c

    lax.fori_loop(0, pieces, piece, 0)
    for b in range(blocks):
        out_ref[:, b * blk : (b + 1) * blk] = acc[b].astype(BF16)


def shards(features, adj_values, neighbours, counts, labels, layer_weight, label_embed):
    fin_dev, slab_nodes = features.shape
    blocks, slots, blk, _ = adj_values.shape
    fin, fout = layer_weight.shape
    col_count, row_count = lax.axis_size("col"), lax.axis_size("row")
    ny, nz = row_count // NX, col_count // 2
    rows_x, cols_y = fin_dev // NX, fout // ny
    parts = blocks // col_count
    factor = 1.0 / math.sqrt(slab_nodes * row_count)
    in_vmem = pl.BlockSpec(memory_space=pltpu.VMEM)
    in_smem = pl.BlockSpec(memory_space=pltpu.SMEM)
    anywhere = pl.BlockSpec(memory_space=pl.ANY)
    pieces = 4
    dma = pltpu.SemaphoreType.DMA

    returned, weight_grad = pl.pallas_call(
        functools.partial(exchange_kernel, col_count, row_count, factor),
        out_shape=(
            jax.ShapeDtypeStruct((blocks, fin_dev, blk), BF16),
            jax.ShapeDtypeStruct((fin_dev, fout), F32),
        ),
        in_specs=[in_smem, in_smem, in_vmem, in_vmem, in_vmem, anywhere, anywhere],
        out_specs=(anywhere, in_vmem),
        scratch_shapes=[
            pltpu.VMEM((blocks, fin_dev, blk), BF16),
            pltpu.VMEM((parts, col_count, slots * blk, blk), BF16),
            pltpu.VMEM((fin, fout), BF16),
            pltpu.VMEM((parts, col_count, fin_dev, blk), BF16),
            pltpu.VMEM((parts, fin, blk), BF16),
            pltpu.VMEM((parts, blk, fout), BF16),
            pltpu.VMEM((parts, col_count, fin_dev, blk), BF16),
            pltpu.VMEM((nz, 2, fin_dev, fout), F32),
            pltpu.VMEM((nz, fin_dev, fout), BF16),
            pltpu.VMEM((nz, fin_dev, fout), BF16),
            pltpu.VMEM((NX, nz * rows_x, fout), BF16),
            pltpu.VMEM((NX - 1, nz * rows_x, fout), BF16),
            pltpu.VMEM((ny, nz * rows_x, cols_y), F32),
            pltpu.VMEM((ny, nz * rows_x, cols_y), BF16),
            pltpu.VMEM((ny - 1, nz * rows_x, cols_y), BF16),
            pltpu.VMEM((nz, rows_x, cols_y), F32),
            pltpu.VMEM((nz - 1, rows_x, cols_y), F32),
            pltpu.VMEM((ny, rows_x, cols_y), F32),
            pltpu.VMEM((NX, rows_x, fout), F32),
            dma((parts, pieces)),
            dma,
            dma((parts,)),
            dma,
            dma((parts,)),
            dma,
            dma,
            dma((6,)),
            dma((6,)),
        ],
        compiler_params=pltpu.CompilerParams(
            collective_id=0, has_side_effects=True, vmem_limit_bytes=VMEM_LIMIT
        ),
        name="exchange",
    )(
        neighbours,
        counts,
        features,
        labels.reshape(blocks, blk),
        label_embed,
        adj_values.reshape(col_count, parts, slots * blk, blk),
        layer_weight,
    )

    spread_pieces = 12
    feature_grad = pl.pallas_call(
        spread_kernel,
        out_shape=jax.ShapeDtypeStruct((fin_dev, slab_nodes), BF16),
        in_specs=[in_smem, in_smem, in_vmem, anywhere],
        out_specs=in_vmem,
        scratch_shapes=[
            pltpu.VMEM((blocks, slots * blk, blk), BF16),
            pltpu.VMEM((blocks, fin_dev, blk), F32),
            dma((spread_pieces,)),
        ],
        compiler_params=pltpu.CompilerParams(vmem_limit_bytes=VMEM_LIMIT),
        name="spread",
    )(neighbours, counts, returned, adj_values.reshape(blocks, slots * blk, blk))
    return weight_grad, feature_grad


def solution(mesh):
    return jax.shard_map(
        shards,
        mesh=mesh,
        in_specs=(
            P("col", "row"),
            P("row", None, None, None),
            P("row", None),
            P("row"),
            P("row"),
            P(),
            P(),
        ),
        out_specs=(P("col", None), P("col", "row")),
        check_vma=False,
    )
```

time: 586 us -> 92.8 us (0.16)
  the two profiles are of different devices: /device:TPU:1 before, /device:TPU:8 now
where the time goes in v1:
time: 92.8 us; the launch traced here: 92.5 us
  Pallas kernels  89.8 us (97%)
  local copies, waits for them, and re-layouts  2.05 us (2%)
    pallas_call x1, Pallas kernels, shards(): pl.pallas_call(functools.partial(exchange_kernel, col_count, row_count, f...  81.7 us
    pallas_call x1, Pallas kernels, shards(): pl.pallas_call(spread_kernel, out_shape=jax.ShapeDtypeStruct((fin_dev, sl...  8.08 us
    unnamed x4, local copies, waits for them, and re-layouts  2.05 us

profile of v1, /device:TPU:8, one launch (start us, length us, event | category | flops | bytes accessed | tf_op | source)
XLA Modules:
  0.0 92.5 jit_solution(6126279374771270604)
XLA Ops:
  0.6 1.4 %copy.9.nbr_ref = s32[72,4]{1,0:T(8,128)} copy(s32[72,4]{0,1:T(4,128)} %param.9) | data formatting | bytes 2304 | tf_op args[2]
  2.0 81.7 %exchange.1 = (bf16[72,32,128]{2,1,0:T(8,128)(2,1)}, f32[32,1024]{1,0:T(8,128)}) custom-call(s32[72,4]{1,0:T(8,128)} %copy.9.nbr_ref, s32[72]{0:T(128)} %cnt_ref.3, bf16[32,9216]{1,0:T(8,128)(2,1)} %x_ref.1, s32[72,128]{1,0:T(8,128)} %bitcast.5, bf16[153,1024]{1,0:T(8,128)(2,1)} %le_ref.1, bf16[24,3,512,128]{3,2,1,0:T(8,128)(2,1)} %bitcast.3, ...), custom_call_target="tpu_custom_call" | custom-call | tf_op jit(solution)/shard_map/exchange/pallas_call | solution.py:405
  83.8 0.0 copy-start
  83.8 8.1 %spread.1 = bf16[32,9216]{1,0:T(8,128)(2,1)} custom-call(s32[72,4]{1,0:T(8,128)} %copy.9.nbr_ref, s32[72]{0:T(128)} %cnt_ref.3, bf16[72,32,128]{2,1,0:T(8,128)(2,1)} %get-tuple-element.5.ga_ref, bf16[72,512,128]{2,1,0:T(8,128)(2,1)} %bitcast.4), custom_call_target="tpu_custom_call" | custom-call | tf_op jit(solution)/shard_map/spread/pallas_call | solution.py:458
  91.9 0.0 copy-done
  91.9 0.7 copy.12
Async XLA Ops:
  83.8 8.1 %copy-start = (f32[32,1024]{1,0:T(8,128)S(1)}, f32[32,1024]{1,0:T(8,128)}, u32[]{:S(2)}) copy-start(f32[32,1024]{1,0:T(8,128)} %get-tuple-element.8) | copy-start | bytes 393220

commit v2 on v1

v2 whole, which is shorter than its diff:
```python
import functools
import math

import jax
import jax.numpy as jnp
from jax import lax
from jax.experimental import pallas as pl
from jax.experimental.pallas import tpu as pltpu
from jax.sharding import PartitionSpec as P

NX = 4
BF16, F32 = jnp.bfloat16, jnp.float32
MESH = pl.DeviceIdType.MESH
VMEM_LIMIT = 56 * 1024 * 1024


def exchange_kernel(
    col_count,
    row_count,
    factor,
    nbr_ref,
    cnt_ref,
    nbr_rows,
    cnt_row,
    x_ref,
    lab_ref,
    le_ref,
    adj_hbm,
    w_hbm,
    wg_ref,
    fg_ref,
    x_blocks,
    adj,
    w,
    agg,
    rg,
    gh,
    ga,
    ret,
    one_hots,
    terms,
    total_f,
    wp,
    core_out,
    core_in,
    x_out,
    x_in,
    q_own,
    y_out,
    y_in,
    z_out,
    z_in,
    y_all,
    x_all,
    adj_sem,
    w_sem,
    fwd_send,
    fwd_recv,
    bwd_send,
    bwd_recv,
    red_send,
    red_recv,
    last_send,
    last_recv,
):
    parts = agg.shape[0]
    fin_dev = x_ref.shape[0]
    fin, fout = w.shape
    slots = nbr_ref.shape[0]
    blocks = nbr_ref.shape[1]
    blk = x_ref.shape[1] // blocks
    ny, nz = row_count // NX, col_count // 2
    rows_x, cols_y = fin_dev // NX, fout // ny
    classes = le_ref.shape[0]

    col, row = lax.axis_index("col"), lax.axis_index("row")
    z, core = col // 2, lax.rem(col, 2)
    y, x = row // NX, lax.rem(row, NX)

    def col_peer(s):
        return lax.rem(col + s, col_count)

    def x_peer(s):
        return y * NX + lax.rem(x + s, NX)

    def y_peer(s):
        return lax.rem(y + s, ny) * NX + x

    barrier = pltpu.get_barrier_semaphore()

    def greet_col(s, c):
        pl.semaphore_signal(barrier, inc=1, device_id={"col": col_peer(s)}, device_id_type=MESH)
        return c

    lax.fori_loop(1, col_count, greet_col, 0)
    for s in range(1, NX):
        pl.semaphore_signal(barrier, inc=1, device_id={"row": x_peer(s)}, device_id_type=MESH)
    for s in range(1, ny):
        pl.semaphore_signal(barrier, inc=1, device_id={"row": y_peer(s)}, device_id_type=MESH)

    pieces = adj_sem.shape[1]
    width = col_count // pieces

    def adj_copy(b, g):
        at = pl.ds(g * width, width)
        return pltpu.make_async_copy(adj_hbm.at[b, at], adj.at[b, at], adj_sem.at[b, g])

    for b in range(parts):
        for g in range(pieces):
            adj_copy(b, g).start()
    w_copy = pltpu.make_async_copy(w_hbm, w, w_sem)
    w_copy.start()

    for k in range(blocks):
        x_blocks[k] = x_ref[:, k * blk : (k + 1) * blk]

    def aggregate(b, g):
        adj_copy(b, g).wait()

        def one(d, c):
            i = b * col_count + d
            count = cnt_ref[i]
            picked = []
            for k in range(slots):
                live = jnp.clip(count - k, 0, 1).astype(F32)
                picked.append(x_blocks[nbr_ref[k, i]] * jnp.full((fin_dev, blk), live).astype(BF16))
            total = jnp.dot(
                jnp.concatenate(picked, axis=1), adj[b, d], preferred_element_type=F32
            )
            agg[b, d] = total.astype(BF16)
            return c

        for t in range(width):
            one(g * width + t, 0)

    def send_forward(b):
        def one(s, c):
            d = col_peer(s)
            pltpu.make_async_remote_copy(
                agg.at[b, d],
                rg.at[b, pl.ds(col * fin_dev, fin_dev)],
                fwd_send,
                fwd_recv.at[b],
                device_id={"col": d},
                device_id_type=MESH,
            ).start()
            return c

        lax.fori_loop(1, col_count, one, 0)

    for b in range(parts):
        lax.fori_loop(0, pieces, lambda g, c, b=b: (aggregate(b, g), c)[1], 0)
        if b == 0:
            pl.semaphore_wait(barrier, (col_count - 1) + (NX - 1) + (ny - 1))
        send_forward(b)
        rg[b, pl.ds(pl.multiple_of(col * fin_dev, fin_dev), fin_dev), :] = agg[b, col]

    square = (blocks, blocks)
    diagonal = lax.broadcasted_iota(jnp.int32, square, 0) == lax.broadcasted_iota(jnp.int32, square, 1)
    goes_to = []
    for k in range(slots):
        line = jnp.where(cnt_row[...] > k, nbr_rows[k : k + 1, :] + 1, 0).astype(F32)
        goes_to.append(jnp.sum(jnp.where(diagonal, line, 0.0), axis=1, keepdims=True))
    for b in range(parts):
        wide = (blocks, one_hots.shape[2])
        source = lax.broadcasted_iota(jnp.int32, wide, 0)
        lane = lax.broadcasted_iota(jnp.int32, wide, 1)
        line = jnp.zeros((1, wide[1]), F32)
        for h in range(2):
            for k in range(slots):
                low = (h * slots + k) * col_count
                here = (source - b * col_count == lane - low) & (lane >= low)
                here = here & (lane < low + col_count)
                line = line + jnp.sum(jnp.where(here, goes_to[k], 0.0), axis=0, keepdims=True)
        target = lax.broadcasted_iota(jnp.int32, one_hots.shape[1:], 0).astype(F32) + 1.0
        one_hots[b] = jnp.where(target == line, 1.0, 0.0).astype(BF16)

    w_copy.wait()
    tile = min(256, fout)

    def node_part(b, c):
        got = rg.at[b, pl.ds(0, fin - fin_dev)]
        pltpu.make_async_copy(got, got, fwd_recv.at[b]).wait()
        rows = rg[b]
        label = lab_ref[pl.ds(b * col_count + col, 1), :]
        one_hot = jnp.where(
            lax.broadcasted_iota(jnp.int32, (classes, blk), 0) == label, 1.0, 0.0
        ).astype(BF16)
        for j in range(fout // tile):
            at = pl.ds(j * tile, tile)
            hidden = lax.dot_general(
                rows, w[:, at], (((0,), (0,)), ((), ())), preferred_element_type=F32
            )
            target = lax.dot_general(
                one_hot, le_ref[:, at], (((0,), (0,)), ((), ())), preferred_element_type=F32
            )
            sigma = 1.0 / (1.0 + jnp.exp(-hidden))
            slope = sigma * (1.0 + hidden * (1.0 - sigma))
            gh[b, :, at] = (slope * target).astype(BF16)
        grad = gh[b]
        step = min(256, fin)
        for m in range(fin // step):
            part = lax.dot_general(
                w[pl.ds(m * step, step), :],
                grad,
                (((1,), (1,)), ((), ())),
                preferred_element_type=F32,
            ).astype(BF16)
            per = step // fin_dev
            ga[b, pl.ds(m * per, per)] = part.reshape(per, fin_dev, blk)

        def send(s, c):
            d = col_peer(s)
            pltpu.make_async_remote_copy(
                ga.at[b, d],
                ret.at[b, col],
                bwd_send,
                bwd_recv.at[b],
                device_id={"col": d},
                device_id_type=MESH,
            ).start()
            return c

        lax.fori_loop(1, col_count, send, 0)
        ret[b, col] = ga[b, col]
        return c

    lax.fori_loop(0, parts, node_part, 0)

    entries = slots * col_count
    f_rows = total_f.shape[0] // fin_dev

    def spread(b):
        got = ret.at[b, pl.ds(0, col_count - 1)]
        pltpu.make_async_copy(got, got, bwd_recv.at[b]).wait()
        group = 4

        def make(g, c):
            for t in range(group):
                d = g * group + t
                term = lax.dot_general(
                    ret[b, d], adj[b, d], (((1,), (1,)), ((), ())), preferred_element_type=F32
                )
                for k in range(slots):
                    at = pl.multiple_of((k * col_count + d) * fin_dev, fin_dev)
                    terms[pl.ds(at, fin_dev), :] = term[:, k * blk : (k + 1) * blk]
            return c

        lax.fori_loop(0, col_count // group, make, 0)
        table = one_hots[b]

        def add(p, c):
            for t in range(2):
                f = (p * 2 + t) * 2
                term = jnp.concatenate(
                    [terms[pl.ds(f + h, entries, stride=fin_dev), :] for h in range(2)], axis=1
                )
                high = term.astype(BF16)
                low = (term - high.astype(F32)).astype(BF16)
                part = jnp.dot(
                    table, jnp.concatenate([high, low], axis=0), preferred_element_type=F32
                )
                for h in range(2):
                    at = pl.ds(pl.multiple_of((f + h) * f_rows, 8), f_rows)
                    piece = part[:, h * blk : (h + 1) * blk]
                    total_f[at, :] = piece if b == 0 else total_f[at, :] + piece
            return c

        lax.fori_loop(0, fin_dev // 4, add, 0)

    chunks, zc = core_out.shape[0], core_out.shape[1]
    pair = 16 // rows_x
    rows_c = zc * 2 * fin_dev

    def weight_part(g):
        at = pl.ds(g * rows_c, rows_c)
        left = jnp.concatenate([rg[b, at, :] for b in range(parts)], axis=1)

        def columns(j, c):
            at = pl.ds(pl.multiple_of(j * tile, tile), tile)
            right = jnp.concatenate([gh[b, :, at] for b in range(parts)], axis=0)
            part = jnp.dot(left, right, preferred_element_type=F32)
            wp[g, :, :, :, at] = part.reshape(zc, 2, fin_dev, tile)
            return c

        lax.fori_loop(0, fout // tile, columns, 0)

        def round_core(i, c):
            core_out[g, i] = wp[g, i, 1 - core].astype(BF16)
            return c

        lax.fori_loop(0, zc, round_core, 0)

    def to_core(g):
        return pltpu.make_async_remote_copy(
            core_out.at[g],
            core_in.at[g],
            red_send.at[0, g],
            red_recv.at[0, g],
            device_id={"col": z * 2 + 1 - core},
            device_id_type=MESH,
        )

    def send_x(g):
        to_core(g).wait_recv()

        def round_x(i, c):
            sums = []
            for t in range(pair):
                total = wp[g, i * pair + t, core] + core_in[g, i * pair + t].astype(F32)
                wp[g, i * pair + t, core] = total
                sums.append(total)
            for k in range(NX):
                piece = jnp.concatenate([v[k * rows_x : (k + 1) * rows_x] for v in sums], axis=0)
                x_out[g, k, pl.ds(pl.multiple_of(i * 16, 16), 16), :] = piece.astype(BF16)
            return c

        lax.fori_loop(0, zc // pair, round_x, 0)
        for s in range(1, NX):
            pltpu.make_async_remote_copy(
                x_out.at[g, lax.rem(x + s, NX)],
                x_in.at[g, s - 1],
                red_send.at[1, g],
                red_recv.at[1, g],
                device_id={"row": x_peer(s)},
                device_id_type=MESH,
            ).start()

    def send_y(g):
        pltpu.make_async_copy(x_in.at[g], x_in.at[g], red_recv.at[1, g]).wait()

        def round_y(i, c):
            at = pl.ds(pl.multiple_of(i * 16, 16), 16)
            own = pl.ds(pl.multiple_of(x * rows_x, rows_x), rows_x)
            total = jnp.concatenate(
                [wp[g, i * pair + t, core, own, :] for t in range(pair)], axis=0
            )
            for s in range(NX - 1):
                total = total + x_in[g, s, at, :].astype(F32)
            for k in range(ny):
                piece = total[:, k * cols_y : (k + 1) * cols_y]
                q_own[g, k, at, :] = piece
                y_out[g, k, at, :] = piece.astype(BF16)
            return c

        lax.fori_loop(0, zc // pair, round_y, 0)

        def one(s, c):
            pltpu.make_async_remote_copy(
                y_out.at[g, lax.rem(y + s, ny)],
                y_in.at[g, s - 1],
                red_send.at[2, g],
                red_recv.at[2, g],
                device_id={"row": y_peer(s)},
                device_id_type=MESH,
            ).start()
            return c

        lax.fori_loop(1, ny, one, 0)

    for g in range(chunks):
        weight_part(g)
        to_core(g).start()
        if g > 0:
            send_x(g - 1)
    send_x(chunks - 1)
    spread(0)
    for g in range(chunks):
        send_y(g)

    for g in range(chunks):
        pltpu.make_async_copy(y_in.at[g], y_in.at[g], red_recv.at[2, g]).wait()
        total = q_own[g, y]
        for s in range(ny - 1):
            total = total + y_in[g, s].astype(F32)
        z_out[g * zc : (g + 1) * zc] = total.reshape(zc, rows_x, cols_y)

    def send_z(s, c):
        other = lax.rem(z + s, nz)
        pltpu.make_async_remote_copy(
            z_out.at[other],
            z_in.at[s - 1],
            last_send.at[0],
            last_recv.at[0],
            device_id={"col": other * 2 + core},
            device_id_type=MESH,
        ).start()
        return c

    lax.fori_loop(1, nz, send_z, 0)
    for b in range(1, parts - 1):
        spread(b)
    pltpu.make_async_copy(z_in, z_in, last_recv.at[0]).wait()
    total = z_out[z]
    for s in range(nz - 1):
        total = total + z_in[s]
    y_all[y] = total * factor

    def share_y(s, c):
        pltpu.make_async_remote_copy(
            y_all.at[y],
            y_all.at[y],
            last_send.at[1],
            last_recv.at[1],
            device_id={"row": y_peer(s)},
            device_id_type=MESH,
        ).start()
        return c

    lax.fori_loop(1, ny, share_y, 0)
    spread(parts - 1)
    got = y_all.at[pl.ds(0, ny - 1)]
    pltpu.make_async_copy(got, got, last_recv.at[1]).wait()
    x_all[x] = jnp.concatenate([y_all[k] for k in range(ny)], axis=1)
    for s in range(1, NX):
        pltpu.make_async_remote_copy(
            x_all.at[x],
            x_all.at[x],
            last_send.at[2],
            last_recv.at[2],
            device_id={"row": x_peer(s)},
            device_id_type=MESH,
        ).start()
    for k in range(blocks):
        grad = total_f[pl.ds(k, fin_dev, stride=f_rows), :]
        fg_ref[:, k * blk : (k + 1) * blk] = grad.astype(BF16)
    got = x_all.at[pl.ds(0, NX - 1)]
    pltpu.make_async_copy(got, got, last_recv.at[2]).wait()
    wg_ref[...] = x_all[...].reshape(fin_dev, fout)

    sent = agg.at[:, pl.ds(0, col_count - 1)]
    pltpu.make_async_copy(sent, sent, fwd_send).wait()
    sent = ga.at[:, pl.ds(0, col_count - 1)]
    pltpu.make_async_copy(sent, sent, bwd_send).wait()
    for g in range(chunks):
        to_core(g).wait_send()
        pltpu.make_async_copy(x_in.at[g], x_in.at[g], red_send.at[1, g]).wait()
        pltpu.make_async_copy(y_in.at[g], y_in.at[g], red_send.at[2, g]).wait()
    pltpu.make_async_copy(z_in, z_in, last_send.at[0]).wait()
    sent = y_all.at[pl.ds(0, ny - 1)]
    pltpu.make_async_copy(sent, sent, last_send.at[1]).wait()
    sent = x_all.at[pl.ds(0, NX - 1)]
    pltpu.make_async_copy(sent, sent, last_send.at[2]).wait()


def shards(features, adj_values, neighbours, counts, labels, layer_weight, label_embed):
    fin_dev, slab_nodes = features.shape
    blocks, slots, blk, _ = adj_values.shape
    fin, fout = layer_weight.shape
    col_count, row_count = lax.axis_size("col"), lax.axis_size("row")
    ny, nz = row_count // NX, col_count // 2
    rows_x, cols_y = fin_dev // NX, fout // ny
    parts = blocks // col_count
    factor = 1.0 / math.sqrt(slab_nodes * row_count)
    in_vmem = pl.BlockSpec(memory_space=pltpu.VMEM)
    in_smem = pl.BlockSpec(memory_space=pltpu.SMEM)
    anywhere = pl.BlockSpec(memory_space=pl.ANY)
    pieces = 4
    zc = 4 if nz % 4 == 0 and nz > 4 else 2
    chunks = nz // zc
    rows_c = zc * rows_x
    f_rows = -(-blocks // 16) * 16
    dma = pltpu.SemaphoreType.DMA

    return pl.pallas_call(
        functools.partial(exchange_kernel, col_count, row_count, factor),
        out_shape=(
            jax.ShapeDtypeStruct((fin_dev, fout), F32),
            jax.ShapeDtypeStruct((fin_dev, slab_nodes), BF16),
        ),
        in_specs=[in_smem] * 2 + [in_vmem] * 5 + [anywhere] * 2,
        out_specs=(in_vmem, in_vmem),
        scratch_shapes=[
            pltpu.VMEM((blocks, fin_dev, blk), BF16),
            pltpu.VMEM((parts, col_count, slots * blk, blk), BF16),
            pltpu.VMEM((fin, fout), BF16),
            pltpu.VMEM((parts, col_count, fin_dev, blk), BF16),
            pltpu.VMEM((parts, fin, blk), BF16),
            pltpu.VMEM((parts, blk, fout), BF16),
            pltpu.VMEM((parts, col_count, fin_dev, blk), BF16),
            pltpu.VMEM((parts, col_count, fin_dev, blk), BF16),
            pltpu.VMEM((parts, f_rows, 2 * slots * col_count), BF16),
            pltpu.VMEM((slots * col_count * fin_dev, blk), F32),
            pltpu.VMEM((fin_dev * f_rows, blk), F32),
            pltpu.VMEM((chunks, zc, 2, fin_dev, fout), F32),
            pltpu.VMEM((chunks, zc, fin_dev, fout), BF16),
            pltpu.VMEM((chunks, zc, fin_dev, fout), BF16),
            pltpu.VMEM((chunks, NX, rows_c, fout), BF16),
            pltpu.VMEM((chunks, NX - 1, rows_c, fout), BF16),
            pltpu.VMEM((chunks, ny, rows_c, cols_y), F32),
            pltpu.VMEM((chunks, ny, rows_c, cols_y), BF16),
            pltpu.VMEM((chunks, ny - 1, rows_c, cols_y), BF16),
            pltpu.VMEM((nz, rows_x, cols_y), F32),
            pltpu.VMEM((nz - 1, rows_x, cols_y), F32),
            pltpu.VMEM((ny, rows_x, cols_y), F32),
            pltpu.VMEM((NX, rows_x, fout), F32),
            dma((parts, pieces)),
            dma,
            dma,
            dma((parts,)),
            dma,
            dma((parts,)),
            dma((3, chunks)),
            dma((3, chunks)),
            dma((3,)),
            dma((3,)),
        ],
        compiler_params=pltpu.CompilerParams(
            collective_id=0, has_side_effects=True, vmem_limit_bytes=VMEM_LIMIT
        ),
        name="exchange",
    )(
        neighbours.T,
        counts,
        neighbours.T,
        counts.reshape(1, blocks),
        features,
        labels.reshape(blocks, blk),
        label_embed,
        adj_values.reshape(parts, col_count, slots * blk, blk),
        layer_weight,
    )


def solution(mesh):
    return jax.shard_map(
        shards,
        mesh=mesh,
        in_specs=(
            P("col", "row"),
            P("row", None, None, None),
            P("row", None),
            P("row"),
            P("row"),
            P(),
            P(),
        ),
        out_specs=(P("col", None), P("col", "row")),
        check_vma=False,
    )
```

time: 92.8 us -> 82.3 us (0.89)
  the two profiles are of different devices: /device:TPU:8 before, /device:TPU:1 now
where the time goes in v2:
time: 82.3 us; the launch traced here: 81.2 us
  Pallas kernels  77.1 us (94%)
  local copies, waits for them, and re-layouts  3.48 us (4%)
    pallas_call x1, Pallas kernels, shards(): pl.pallas_call(functools.partial(exchange_kernel, col_count, row_count, f...  77.1 us
    unnamed x2, local copies, waits for them, and re-layouts  3.48 us

profile of v2, /device:TPU:1, one launch (start us, length us, event | category | flops | bytes accessed | tf_op | source)
XLA Modules:
  0.0 81.2 jit_solution(10574020200026634315)
XLA Ops:
  0.6 77.1 %exchange.1 = (f32[32,1024]{1,0:T(8,128)}, bf16[32,9216]{1,0:T(8,128)(2,1)}) custom-call(s32[4,72]{1,0:T(4,128)} %bitcast.6, s32[72]{0:T(128)} %cnt_ref.1, s32[4,72]{1,0:T(4,128)} %bitcast.7, s32[1,72]{1,0:T(1,128)} %bitcast.8, bf16[32,9216]{1,0:T(8,128)(2,1)} %x_ref.1, s32[72,128]{1,0:T(8,128)} %bitcast.5, bf16[153,1024]{1,0:T(8,128)(2,1)} %le_ref.1, ...), custom_call_target="tpu_custom_call" | custom-call | tf_op jit(solution)/shard_map/exchange/pallas_call | solution.py:465
  77.7 1.6 %copy.11 = f32[32,1024]{1,0:T(8,128)} copy(f32[32,1024]{1,0:T(8,128)} %get-tuple-element.4) | data formatting | bytes 262144
  79.3 1.9 %copy.12 = bf16[32,9216]{1,0:T(8,128)(2,1)} copy(bf16[32,9216]{1,0:T(8,128)(2,1)} %get-tuple-element.5) | data formatting | bytes 1179648

commit v3 on v2

--- a/solution.py
+++ b/solution.py
@@ -50,8 +50,7 @@
     y_in,
     z_out,
     z_in,
-    y_all,
-    x_all,
+    shared,
     adj_sem,
     w_sem,
     fwd_send,
@@ -83,6 +82,9 @@
     def x_peer(s):
         return y * NX + lax.rem(x + s, NX)
 
+    def row_peer(s):
+        return lax.rem(row + s, row_count)
+
     def y_peer(s):
         return lax.rem(y + s, ny) * NX + x
 
@@ -93,10 +95,11 @@
         return c
 
     lax.fori_loop(1, col_count, greet_col, 0)
-    for s in range(1, NX):
-        pl.semaphore_signal(barrier, inc=1, device_id={"row": x_peer(s)}, device_id_type=MESH)
-    for s in range(1, ny):
-        pl.semaphore_signal(barrier, inc=1, device_id={"row": y_peer(s)}, device_id_type=MESH)
+    def greet_row(s, c):
+        pl.semaphore_signal(barrier, inc=1, device_id={"row": row_peer(s)}, device_id_type=MESH)
+        return c
+
+    lax.fori_loop(1, row_count, greet_row, 0)
 
     pieces = adj_sem.shape[1]
     width = col_count // pieces
@@ -105,9 +108,12 @@
         at = pl.ds(g * width, width)
         return pltpu.make_async_copy(adj_hbm.at[b, at], adj.at[b, at], adj_sem.at[b, g])
 
+    def group(g):
+        return lax.rem(col // width + g, pieces)
+
     for b in range(parts):
         for g in range(pieces):
-            adj_copy(b, g).start()
+            adj_copy(b, group(g)).start()
     w_copy = pltpu.make_async_copy(w_hbm, w, w_sem)
     w_copy.start()
 
@@ -133,26 +139,36 @@
         for t in range(width):
             one(g * width + t, 0)
 
-    def send_forward(b):
-        def one(s, c):
-            d = col_peer(s)
-            pltpu.make_async_remote_copy(
-                agg.at[b, d],
-                rg.at[b, pl.ds(col * fin_dev, fin_dev)],
-                fwd_send,
-                fwd_recv.at[b],
-                device_id={"col": d},
-                device_id_type=MESH,
-            ).start()
-            return c
-
-        lax.fori_loop(1, col_count, one, 0)
-
+    def send_forward(b, g):
+        def one(t, c):
+            d = g * width + lax.rem(col + t, width)
+
+            @pl.when(d != col)
+            def _():
+                pltpu.make_async_remote_copy(
+                    agg.at[b, d],
+                    rg.at[b, pl.ds(col * fin_dev, fin_dev)],
+                    fwd_send,
+                    fwd_recv.at[b],
+                    device_id={"col": d},
+                    device_id_type=MESH,
+                ).start()
+
+            return c
+
+        lax.fori_loop(0, width, one, 0)
+
+    aggregate(0, group(0))
+    pl.semaphore_wait(barrier, (col_count - 1) + (row_count - 1))
+    send_forward(0, group(0))
     for b in range(parts):
-        lax.fori_loop(0, pieces, lambda g, c, b=b: (aggregate(b, g), c)[1], 0)
-        if b == 0:
-            pl.semaphore_wait(barrier, (col_count - 1) + (NX - 1) + (ny - 1))
-        send_forward(b)
+
+        def both(g, c, b=b):
+            aggregate(b, group(g))
+            send_forward(b, group(g))
+            return c
+
+        lax.fori_loop(1 if b == 0 else 0, pieces, both, 0)
         rg[b, pl.ds(pl.multiple_of(col * fin_dev, fin_dev), fin_dev), :] = agg[b, col]
 
     square = (blocks, blocks)
@@ -233,11 +249,11 @@
     def spread(b):
         got = ret.at[b, pl.ds(0, col_count - 1)]
         pltpu.make_async_copy(got, got, bwd_recv.at[b]).wait()
-        group = 4
+        several = 4
 
         def make(g, c):
-            for t in range(group):
-                d = g * group + t
+            for t in range(several):
+                d = g * several + t
                 term = lax.dot_general(
                     ret[b, d], adj[b, d], (((1,), (1,)), ((), ())), preferred_element_type=F32
                 )
@@ -246,7 +262,7 @@
                     terms[pl.ds(at, fin_dev), :] = term[:, k * blk : (k + 1) * blk]
             return c
 
-        lax.fori_loop(0, col_count // group, make, 0)
+        lax.fori_loop(0, col_count // several, make, 0)
         table = one_hots[b]
 
         def add(p, c):
@@ -367,6 +383,8 @@
     spread(0)
     for g in range(chunks):
         send_y(g)
+    for b in range(1, parts - 1):
+        spread(b)
 
     for g in range(chunks):
         pltpu.make_async_copy(y_in.at[g], y_in.at[g], red_recv.at[2, g]).wait()
@@ -388,45 +406,34 @@
         return c
 
     lax.fori_loop(1, nz, send_z, 0)
-    for b in range(1, parts - 1):
-        spread(b)
+    spread(parts - 1)
     pltpu.make_async_copy(z_in, z_in, last_recv.at[0]).wait()
     total = z_out[z]
     for s in range(nz - 1):
         total = total + z_in[s]
-    y_all[y] = total * factor
-
-    def share_y(s, c):
+    shared[row] = total * factor
+
+    def share(s, c):
         pltpu.make_async_remote_copy(
-            y_all.at[y],
-            y_all.at[y],
+            shared.at[row],
+            shared.at[row],
             last_send.at[1],
             last_recv.at[1],
-            device_id={"row": y_peer(s)},
+            device_id={"row": row_peer(s)},
             device_id_type=MESH,
         ).start()
         return c
 
-    lax.fori_loop(1, ny, share_y, 0)
-    spread(parts - 1)
-    got = y_all.at[pl.ds(0, ny - 1)]
-    pltpu.make_async_copy(got, got, last_recv.at[1]).wait()
-    x_all[x] = jnp.concatenate([y_all[k] for k in range(ny)], axis=1)
-    for s in range(1, NX):
-        pltpu.make_async_remote_copy(
-            x_all.at[x],
-            x_all.at[x],
-            last_send.at[2],
-            last_recv.at[2],
-            device_id={"row": x_peer(s)},
-            device_id_type=MESH,
-        ).start()
+    lax.fori_loop(1, row_count, share, 0)
     for k in range(blocks):
         grad = total_f[pl.ds(k, fin_dev, stride=f_rows), :]
         fg_ref[:, k * blk : (k + 1) * blk] = grad.astype(BF16)
-    got = x_all.at[pl.ds(0, NX - 1)]
-    pltpu.make_async_copy(got, got, last_recv.at[2]).wait()
-    wg_ref[...] = x_all[...].reshape(fin_dev, fout)
+    got = shared.at[pl.ds(0, row_count - 1)]
+    pltpu.make_async_copy(got, got, last_recv.at[1]).wait()
+    for k in range(NX):
+        wg_ref[k * rows_x : (k + 1) * rows_x, :] = jnp.concatenate(
+            [shared[t * NX + k] for t in range(ny)], axis=1
+        )
 
     sent = agg.at[:, pl.ds(0, col_count - 1)]
     pltpu.make_async_copy(sent, sent, fwd_send).wait()
@@ -437,10 +444,17 @@
         pltpu.make_async_copy(x_in.at[g], x_in.at[g], red_send.at[1, g]).wait()
         pltpu.make_async_copy(y_in.at[g], y_in.at[g], red_send.at[2, g]).wait()
     pltpu.make_async_copy(z_in, z_in, last_send.at[0]).wait()
-    sent = y_all.at[pl.ds(0, ny - 1)]
+    sent = shared.at[pl.ds(0, row_count - 1)]
     pltpu.make_async_copy(sent, sent, last_send.at[1]).wait()
-    sent = x_all.at[pl.ds(0, NX - 1)]
-    pltpu.make_async_copy(sent, sent, last_send.at[2]).wait()
+
+
+def write_kernel(wg_ref, fg_ref, wg_out, fg_out, sems):
+    first = pltpu.make_async_copy(wg_ref, wg_out, sems.at[0])
+    second = pltpu.make_async_copy(fg_ref, fg_out, sems.at[1])
+    first.start()
+    second.start()
+    first.wait()
+    second.wait()
 
 
 def shards(features, adj_values, neighbours, counts, labels, layer_weight, label_embed):
@@ -462,7 +476,7 @@
     f_rows = -(-blocks // 16) * 16
     dma = pltpu.SemaphoreType.DMA
 
-    return pl.pallas_call(
+    weight_grad, feature_grad = pl.pallas_call(
         functools.partial(exchange_kernel, col_count, row_count, factor),
         out_shape=(
             jax.ShapeDtypeStruct((fin_dev, fout), F32),
@@ -492,8 +506,7 @@
             pltpu.VMEM((chunks, ny - 1, rows_c, cols_y), BF16),
             pltpu.VMEM((nz, rows_x, cols_y), F32),
             pltpu.VMEM((nz - 1, rows_x, cols_y), F32),
-            pltpu.VMEM((ny, rows_x, cols_y), F32),
-            pltpu.VMEM((NX, rows_x, fout), F32),
+            pltpu.VMEM((row_count, rows_x, cols_y), F32),
             dma((parts, pieces)),
             dma,
             dma,
@@ -502,8 +515,8 @@
             dma((parts,)),
             dma((3, chunks)),
             dma((3, chunks)),
-            dma((3,)),
-            dma((3,)),
+            dma((2,)),
+            dma((2,)),
         ],
         compiler_params=pltpu.CompilerParams(
             collective_id=0, has_side_effects=True, vmem_limit_bytes=VMEM_LIMIT
@@ -520,6 +533,18 @@
         adj_values.reshape(parts, col_count, slots * blk, blk),
         layer_weight,
     )
+    return pl.pallas_call(
+        write_kernel,
+        out_shape=(
+            jax.ShapeDtypeStruct((fin_dev, fout), F32),
+            jax.ShapeDtypeStruct((fin_dev, slab_nodes), BF16),
+        ),
+        in_specs=[anywhere] * 2,
+        out_specs=(anywhere, anywhere),
+        scratch_shapes=[dma((2,))],
+        compiler_params=pltpu.CompilerParams(vmem_limit_bytes=63 * 1024 * 1024),
+        name="write",
+    )(weight_grad, feature_grad)
 
 
 def solution(mesh):

time: 82.3 us -> 102 us (1.24)
  Pallas kernels: 77.1 us -> 101 us
  local copies, waits for them, and re-layouts: 3.48 us -> 0 us
    pallas_call x0 -> x1, Pallas kernels: none -> 23 us  [shards(): pl.pallas_call(write_kernel, out_shape=(jax.ShapeDtypeStruct((fin_dev, fo...]
    unnamed x2 -> x0, local copies, waits for them, and re-layouts: 3.48 us -> none
where the time goes in v3:
time: 102 us
  Pallas kernels  101 us (99%)
    pallas_call x1, Pallas kernels, shards(): pl.pallas_call(functools.partial(exchange_kernel, col_count, row_count, f...  78 us
    pallas_call x1, Pallas kernels, shards(): pl.pallas_call(write_kernel, out_shape=(jax.ShapeDtypeStruct((fin_dev, fo...  23 us

profile of v3, /device:TPU:1, one launch (start us, length us, event | category | flops | bytes accessed | tf_op | source)
XLA Modules:
  0.0 101.6 jit_solution(3459257892452630240)
XLA Ops:
  0.6 78.0 %exchange.1 = (f32[32,1024]{1,0:T(8,128)}, bf16[32,9216]{1,0:T(8,128)(2,1)}) custom-call(s32[4,72]{1,0:T(4,128)} %bitcast.6, s32[72]{0:T(128)} %cnt_ref.1, s32[4,72]{1,0:T(4,128)} %bitcast.7, s32[1,72]{1,0:T(1,128)} %bitcast.8, bf16[32,9216]{1,0:T(8,128)(2,1)} %x_ref.1, s32[72,128]{1,0:T(8,128)} %bitcast.5, bf16[153,1024]{1,0:T(8,128)(2,1)} %le_ref.1, ...), custom_call_target="tpu_custom_call" | custom-call | tf_op jit(solution)/shard_map/exchange/pallas_call | solution.py:479
  78.7 23.0 %write.1 = (f32[32,1024]{1,0:T(8,128)}, bf16[32,9216]{1,0:T(8,128)(2,1)}) custom-call(f32[32,1024]{1,0:T(8,128)} %get-tuple-element.4.wg_ref, bf16[32,9216]{1,0:T(8,128)(2,1)} %get-tuple-element.5.fg_ref), custom_call_target="tpu_custom_call" | custom-call | tf_op jit(solution)/shard_map/write/pallas_call | solution.py:536

commit v4 on v3

--- a/solution.py
+++ b/solution.py
@@ -48,6 +48,11 @@
     q_own,
     y_out,
     y_in,
+    first_y_out,
+    first_y_in,
+    first_own,
+    first_x_out,
+    first_x_in,
     z_out,
     z_in,
     shared,
@@ -194,7 +199,7 @@
     w_copy.wait()
     tile = min(256, fout)
 
-    def node_part(b, c):
+    def grad_part(b, c):
         got = rg.at[b, pl.ds(0, fin - fin_dev)]
         pltpu.make_async_copy(got, got, fwd_recv.at[b]).wait()
         rows = rg[b]
@@ -213,6 +218,9 @@
             sigma = 1.0 / (1.0 + jnp.exp(-hidden))
             slope = sigma * (1.0 + hidden * (1.0 - sigma))
             gh[b, :, at] = (slope * target).astype(BF16)
+        return c
+
+    def back_part(b, c):
         grad = gh[b]
         step = min(256, fin)
         for m in range(fin // step):
@@ -224,7 +232,10 @@
             ).astype(BF16)
             per = step // fin_dev
             ga[b, pl.ds(m * per, per)] = part.reshape(per, fin_dev, blk)
-
+        ret[b, col] = ga[b, col]
+        return c
+
+    def send_back(b):
         def send(s, c):
             d = col_peer(s)
             pltpu.make_async_remote_copy(
@@ -238,10 +249,16 @@
             return c
 
         lax.fori_loop(1, col_count, send, 0)
-        ret[b, col] = ga[b, col]
+
+    def early(b, c):
+        grad_part(b, c)
+        back_part(b, c)
+        send_back(b)
         return c
 
-    lax.fori_loop(0, parts, node_part, 0)
+    last = parts - 1
+    lax.fori_loop(0, last, early, 0)
+    grad_part(last, 0)
 
     entries = slots * col_count
     f_rows = total_f.shape[0] // fin_dev
@@ -374,19 +391,83 @@
 
         lax.fori_loop(1, ny, one, 0)
 
+    def send_y_first():
+        to_core(0).wait_recv()
+
+        def one_row(i, c):
+            total = wp[0, i, core] + core_in[0, i].astype(F32)
+            wp[0, i, core] = total
+            at = pl.ds(pl.multiple_of(i * fin_dev, fin_dev), fin_dev)
+            for k in range(ny):
+                first_y_out[k, at, :] = total[:, k * cols_y : (k + 1) * cols_y].astype(BF16)
+            return c
+
+        lax.fori_loop(0, zc, one_row, 0)
+
+        def one(s, c):
+            pltpu.make_async_remote_copy(
+                first_y_out.at[lax.rem(y + s, ny)],
+                first_y_in.at[s - 1],
+                red_send.at[2, 0],
+                red_recv.at[2, 0],
+                device_id={"row": y_peer(s)},
+                device_id_type=MESH,
+            ).start()
+            return c
+
+        lax.fori_loop(1, ny, one, 0)
+
+    def send_x_second():
+        pltpu.make_async_copy(first_y_in, first_y_in, red_recv.at[2, 0]).wait()
+
+        def some_rows(i, c):
+            sums = []
+            for t in range(pair):
+                k = i * pair + t
+                total = wp[0, k, core, :, pl.ds(pl.multiple_of(y * cols_y, cols_y), cols_y)]
+                at = pl.ds(pl.multiple_of(k * fin_dev, fin_dev), fin_dev)
+                for s in range(ny - 1):
+                    total = total + first_y_in[s, at, :].astype(F32)
+                sums.append(total)
+            at = pl.ds(pl.multiple_of(i * 16, 16), 16)
+            for k in range(NX):
+                piece = jnp.concatenate([v[k * rows_x : (k + 1) * rows_x] for v in sums], axis=0)
+                first_own[k, at, :] = piece
+                first_x_out[k, at, :] = piece.astype(BF16)
+            return c
+
+        lax.fori_loop(0, zc // pair, some_rows, 0)
+        for s in range(1, NX):
+            pltpu.make_async_remote_copy(
+                first_x_out.at[lax.rem(x + s, NX)],
+                first_x_in.at[s - 1],
+                red_send.at[1, 0],
+                red_recv.at[1, 0],
+                device_id={"row": x_peer(s)},
+                device_id_type=MESH,
+            ).start()
+
     for g in range(chunks):
         weight_part(g)
         to_core(g).start()
-        if g > 0:
+        if g == 1:
+            send_y_first()
+        if g > 1:
             send_x(g - 1)
     send_x(chunks - 1)
+    back_part(last, 0)
+    send_back(last)
     spread(0)
-    for g in range(chunks):
+    send_x_second()
+    for g in range(1, chunks):
         send_y(g)
-    for b in range(1, parts - 1):
-        spread(b)
-
-    for g in range(chunks):
+
+    pltpu.make_async_copy(first_x_in, first_x_in, red_recv.at[1, 0]).wait()
+    total = first_own[x]
+    for s in range(NX - 1):
+        total = total + first_x_in[s].astype(F32)
+    z_out[0:zc] = total.reshape(zc, rows_x, cols_y)
+    for g in range(1, chunks):
         pltpu.make_async_copy(y_in.at[g], y_in.at[g], red_recv.at[2, g]).wait()
         total = q_own[g, y]
         for s in range(ny - 1):
@@ -406,7 +487,8 @@
         return c
 
     lax.fori_loop(1, nz, send_z, 0)
-    spread(parts - 1)
+    for b in range(1, last):
+        spread(b)
     pltpu.make_async_copy(z_in, z_in, last_recv.at[0]).wait()
     total = z_out[z]
     for s in range(nz - 1):
@@ -425,6 +507,7 @@
         return c
 
     lax.fori_loop(1, row_count, share, 0)
+    spread(last)
     for k in range(blocks):
         grad = total_f[pl.ds(k, fin_dev, stride=f_rows), :]
         fg_ref[:, k * blk : (k + 1) * blk] = grad.astype(BF16)
@@ -441,20 +524,18 @@
     pltpu.make_async_copy(sent, sent, bwd_send).wait()
     for g in range(chunks):
         to_core(g).wait_send()
-        pltpu.make_async_copy(x_in.at[g], x_in.at[g], red_send.at[1, g]).wait()
-        pltpu.make_async_copy(y_in.at[g], y_in.at[g], red_send.at[2, g]).wait()
+        left_x = first_x_in if g == 0 else x_in.at[g]
+        left_y = first_y_in if g == 0 else y_in.at[g]
+        pltpu.make_async_copy(left_x, left_x, red_send.at[1, g]).wait()
+        pltpu.make_async_copy(left_y, left_y, red_send.at[2, g]).wait()
     pltpu.make_async_copy(z_in, z_in, last_send.at[0]).wait()
     sent = shared.at[pl.ds(0, row_count - 1)]
     pltpu.make_async_copy(sent, sent, last_send.at[1]).wait()
 
 
-def write_kernel(wg_ref, fg_ref, wg_out, fg_out, sems):
-    first = pltpu.make_async_copy(wg_ref, wg_out, sems.at[0])
-    second = pltpu.make_async_copy(fg_ref, fg_out, sems.at[1])
-    first.start()
-    second.start()
-    first.wait()
-    second.wait()
+def write_kernel(wg_ref, fg_ref, wg_out, fg_out):
+    wg_out[...] = wg_ref[...]
+    fg_out[...] = fg_ref[...]
 
 
 def shards(features, adj_values, neighbours, counts, labels, layer_weight, label_embed):
@@ -504,6 +585,11 @@
             pltpu.VMEM((chunks, ny, rows_c, cols_y), F32),
             pltpu.VMEM((chunks, ny, rows_c, cols_y), BF16),
             pltpu.VMEM((chunks, ny - 1, rows_c, cols_y), BF16),
+            pltpu.VMEM((ny, zc * fin_dev, cols_y), BF16),
+            pltpu.VMEM((ny - 1, zc * fin_dev, cols_y), BF16),
+            pltpu.VMEM((NX, rows_c, cols_y), F32),
+            pltpu.VMEM((NX, rows_c, cols_y), BF16),
+            pltpu.VMEM((NX - 1, rows_c, cols_y), BF16),
             pltpu.VMEM((nz, rows_x, cols_y), F32),
             pltpu.VMEM((nz - 1, rows_x, cols_y), F32),
             pltpu.VMEM((row_count, rows_x, cols_y), F32),
@@ -539,10 +625,8 @@
             jax.ShapeDtypeStruct((fin_dev, fout), F32),
             jax.ShapeDtypeStruct((fin_dev, slab_nodes), BF16),
         ),
-        in_specs=[anywhere] * 2,
-        out_specs=(anywhere, anywhere),
-        scratch_shapes=[dma((2,))],
-        compiler_params=pltpu.CompilerParams(vmem_limit_bytes=63 * 1024 * 1024),
+        in_specs=[in_vmem] * 2,
+        out_specs=(in_vmem, in_vmem),
         name="write",
     )(weight_grad, feature_grad)
 

time: 102 us -> 78.7 us (0.77)
  Pallas kernels: 101 us -> 77.7 us
    pallas_call x1, Pallas kernels: 23 us -> 2.01 us  [shards(): pl.pallas_call(write_kernel, out_shape=(jax.ShapeDtypeStruct((fin_dev, fo...]
    pallas_call x1, Pallas kernels: 78 us -> 75.7 us  [shards(): pl.pallas_call(functools.partial(exchange_kernel, col_count, row_count, f...]
where the time goes in v4:
time: 78.7 us; the launch traced here: 78.3 us
  Pallas kernels  77.7 us (99%)
    pallas_call x1, Pallas kernels, shards(): pl.pallas_call(functools.partial(exchange_kernel, col_count, row_count, f...  75.7 us
    pallas_call x1, Pallas kernels, shards(): pl.pallas_call(write_kernel, out_shape=(jax.ShapeDtypeStruct((fin_dev, fo...  2.01 us

profile of v4, /device:TPU:1, one launch (start us, length us, event | category | flops | bytes accessed | tf_op | source)
XLA Modules:
  0.0 78.3 jit_solution(15889062178076017613)
XLA Ops:
  0.6 75.7 %exchange.1 = (f32[32,1024]{1,0:T(8,128)}, bf16[32,9216]{1,0:T(8,128)(2,1)}) custom-call(s32[4,72]{1,0:T(4,128)} %bitcast.6, s32[72]{0:T(128)} %cnt_ref.1, s32[4,72]{1,0:T(4,128)} %bitcast.7, s32[1,72]{1,0:T(1,128)} %bitcast.8, bf16[32,9216]{1,0:T(8,128)(2,1)} %x_ref.1, s32[72,128]{1,0:T(8,128)} %bitcast.5, bf16[153,1024]{1,0:T(8,128)(2,1)} %le_ref.1, ...), custom_call_target="tpu_custom_call" | custom-call | tf_op jit(solution)/shard_map/exchange/pallas_call | solution.py:560
  76.3 2.0 %write.1 = (f32[32,1024]{1,0:T(8,128)}, bf16[32,9216]{1,0:T(8,128)(2,1)}) custom-call(f32[32,1024]{1,0:T(8,128)} %get-tuple-element.4.wg_ref, bf16[32,9216]{1,0:T(8,128)(2,1)} %get-tuple-element.5.fg_ref), custom_call_target="tpu_custom_call" | custom-call | tf_op jit(solution)/shard_map/write/pallas_call | solution.py:622

commit v5 on v4

--- a/solution.py
+++ b/solution.py
@@ -87,24 +87,14 @@
     def x_peer(s):
         return y * NX + lax.rem(x + s, NX)
 
+    def far_first(t, count):
+        return 1 + lax.rem(t + count // 2 - count // 8 - 1, count - 1)
+
     def row_peer(s):
         return lax.rem(row + s, row_count)
 
     def y_peer(s):
         return lax.rem(y + s, ny) * NX + x
-
-    barrier = pltpu.get_barrier_semaphore()
-
-    def greet_col(s, c):
-        pl.semaphore_signal(barrier, inc=1, device_id={"col": col_peer(s)}, device_id_type=MESH)
-        return c
-
-    lax.fori_loop(1, col_count, greet_col, 0)
-    def greet_row(s, c):
-        pl.semaphore_signal(barrier, inc=1, device_id={"row": row_peer(s)}, device_id_type=MESH)
-        return c
-
-    lax.fori_loop(1, row_count, greet_row, 0)
 
     pieces = adj_sem.shape[1]
     width = col_count // pieces
@@ -121,6 +111,19 @@
             adj_copy(b, group(g)).start()
     w_copy = pltpu.make_async_copy(w_hbm, w, w_sem)
     w_copy.start()
+
+    barrier = pltpu.get_barrier_semaphore()
+
+    def greet_col(s, c):
+        pl.semaphore_signal(barrier, inc=1, device_id={"col": col_peer(s)}, device_id_type=MESH)
+        return c
+
+    lax.fori_loop(1, col_count, greet_col, 0)
+    def greet_row(s, c):
+        pl.semaphore_signal(barrier, inc=1, device_id={"row": row_peer(s)}, device_id_type=MESH)
+        return c
+
+    lax.fori_loop(1, row_count, greet_row, 0)
 
     for k in range(blocks):
         x_blocks[k] = x_ref[:, k * blk : (k + 1) * blk]
@@ -379,6 +382,7 @@
         lax.fori_loop(0, zc // pair, round_y, 0)
 
         def one(s, c):
+            s = far_first(s, ny)
             pltpu.make_async_remote_copy(
                 y_out.at[g, lax.rem(y + s, ny)],
                 y_in.at[g, s - 1],
@@ -405,6 +409,7 @@
         lax.fori_loop(0, zc, one_row, 0)
 
         def one(s, c):
+            s = far_first(s, ny)
             pltpu.make_async_remote_copy(
                 first_y_out.at[lax.rem(y + s, ny)],
                 first_y_in.at[s - 1],
@@ -475,6 +480,7 @@
         z_out[g * zc : (g + 1) * zc] = total.reshape(zc, rows_x, cols_y)
 
     def send_z(s, c):
+        s = far_first(s, nz)
         other = lax.rem(z + s, nz)
         pltpu.make_async_remote_copy(
             z_out.at[other],
@@ -496,6 +502,7 @@
     shared[row] = total * factor
 
     def share(s, c):
+        s = far_first(s, row_count)
         pltpu.make_async_remote_copy(
             shared.at[row],
             shared.at[row],
@@ -533,9 +540,13 @@
     pltpu.make_async_copy(sent, sent, last_send.at[1]).wait()
 
 
-def write_kernel(wg_ref, fg_ref, wg_out, fg_out):
-    wg_out[...] = wg_ref[...]
-    fg_out[...] = fg_ref[...]
+def write_kernel(wg_ref, fg_ref, wg_out, fg_out, sems):
+    first = pltpu.make_async_copy(wg_ref, wg_out, sems.at[0])
+    second = pltpu.make_async_copy(fg_ref, fg_out, sems.at[1])
+    first.start()
+    second.start()
+    first.wait()
+    second.wait()
 
 
 def shards(features, adj_values, neighbours, counts, labels, layer_weight, label_embed):
@@ -626,7 +637,8 @@
             jax.ShapeDtypeStruct((fin_dev, slab_nodes), BF16),
         ),
         in_specs=[in_vmem] * 2,
-        out_specs=(in_vmem, in_vmem),
+        out_specs=(anywhere, anywhere),
+        scratch_shapes=[dma((2,))],
         name="write",
     )(weight_grad, feature_grad)
 

time: 78.7 us -> 78.4 us (level); the launches traced: 78.3 us -> 76.9 us
  Pallas kernels: 77.7 us -> 76.3 us
    pallas_call x1, Pallas kernels: 75.7 us -> 74.3 us  [shards(): pl.pallas_call(functools.partial(exchange_kernel, col_count, row_count, f...]
where the time goes in v5:
time: 78.4 us; the launch traced here: 76.9 us
  Pallas kernels  76.3 us (97%)
    pallas_call x1, Pallas kernels, shards(): pl.pallas_call(functools.partial(exchange_kernel, col_count, row_count, f...  74.3 us
    pallas_call x1, Pallas kernels, shards(): pl.pallas_call(write_kernel, out_shape=(jax.ShapeDtypeStruct((fin_dev, fo...  2.01 us

profile of v5, /device:TPU:1, one launch (start us, length us, event | category | flops | bytes accessed | tf_op | source)
XLA Modules:
  0.0 76.9 jit_solution(17032446181040344696)
XLA Ops:
  0.6 74.3 %exchange.1 = (f32[32,1024]{1,0:T(8,128)}, bf16[32,9216]{1,0:T(8,128)(2,1)}) custom-call(s32[4,72]{1,0:T(4,128)} %bitcast.6, s32[72]{0:T(128)} %cnt_ref.1, s32[4,72]{1,0:T(4,128)} %bitcast.7, s32[1,72]{1,0:T(1,128)} %bitcast.8, bf16[32,9216]{1,0:T(8,128)(2,1)} %x_ref.1, s32[72,128]{1,0:T(8,128)} %bitcast.5, bf16[153,1024]{1,0:T(8,128)(2,1)} %le_ref.1, ...), custom_call_target="tpu_custom_call" | custom-call | tf_op jit(solution)/shard_map/exchange/pallas_call | solution.py:571
  74.9 2.0 %write.1 = (f32[32,1024]{1,0:T(8,128)}, bf16[32,9216]{1,0:T(8,128)(2,1)}) custom-call(f32[32,1024]{1,0:T(8,128)} %get-tuple-element.4.wg_ref, bf16[32,9216]{1,0:T(8,128)(2,1)} %get-tuple-element.5.fg_ref), custom_call_target="tpu_custom_call" | custom-call | tf_op jit(solution)/shard_map/write/pallas_call | solution.py:633
